TPU v7x, 32 devices: a whole 2x2x4 slice. The times are simulated.
32 devices in a mesh: wide: 16 (over z, y, core), narrow: 2 (over x).
Axes of the slice: x: 2, y: 2, z: 4, core: 2. Of those that a mesh axis runs over, the one named last changes fastest.
Arguments:
- initial_warmth_state: float32 [128, 128, 256], P(None, 'wide', 'narrow'), may hold values from -1.5 to 1.5
- diffusivity_coefficient: float32 [128, 128, 256], P(None, 'wide', 'narrow'), may hold values from 0.5 to 8
- heating_supply: float32 [128, 128, 256], P(None, 'wide', 'narrow'), may hold values from -6 to 6
- known_forcing_vector: float32 [128, 128, 256], P(None, 'wide', 'narrow'), as said below
Outputs:
- advanced_warmth_state: float32 [128, 128, 256], P(None, 'wide', 'narrow')
- upcoming_forcing_vector: float32 [128, 128, 256], P(None, 'wide', 'narrow')
Inputs may be any that keep to these rules, and one draw needn't show every extreme that they name: `known_forcing_vector`: values lie within -6 to 6.
All inputs are finite; a program needn't handle non-finite values.
Results may differ from a plain program's by a relative error of at most 0.00035.
Values sent between devices are 32-bit elements; how exact they have to be, the bound alone decides.
A program may use at most 64 MiB of HBM per device.

v0:
```python
import jax
import jax.numpy as jnp
from jax import lax
from jax.sharding import PartitionSpec as P

HALF = 256


def extended(cells, sides, width):
    for axis, dim in sides:
        count = lax.axis_size(axis)
        ends = count - 1
        head = lax.slice_in_dim(cells, 0, width, axis=dim)
        tail = lax.slice_in_dim(cells, cells.shape[dim] - width, cells.shape[dim], axis=dim)
        cells = jnp.concatenate(
            [
                lax.ppermute(tail, axis, [(i, (i + 1) % count) for i in range(ends)]),
                cells,
                lax.ppermute(head, axis, [((i + 1) % count, i) for i in range(ends)]),
            ],
            axis=dim,
        )
    return cells


def solve_lines(below_band, main_band, above_band, right_side):
    length = right_side.shape[0]
    if length == 1:
        return right_side / main_band
    blank = jnp.zeros_like(right_side[:1])
    even_below = below_band[0::2]
    even_main = main_band[0::2]
    even_above = above_band[0::2]
    even_right = right_side[0::2]
    next_below = jnp.concatenate([even_below[1:], blank])
    next_main = jnp.concatenate([even_main[1:], blank + 1.0])
    next_above = jnp.concatenate([even_above[1:], blank])
    next_right = jnp.concatenate([even_right[1:], blank])
    factor_left = -below_band[1::2] / even_main
    factor_right = -above_band[1::2] / next_main
    reduced = solve_lines(
        factor_left * even_below,
        main_band[1::2] + factor_left * even_above + factor_right * next_below,
        factor_right * next_above,
        right_side[1::2] + factor_left * even_right + factor_right * next_right,
    )
    earlier = jnp.concatenate([blank, reduced[:-1]])
    solved_even = (even_right - even_below * earlier - even_above * reduced) / even_main
    return jnp.stack([solved_even, reduced], axis=1).reshape(right_side.shape)


def line_solve(cond, right_side):
    half_ratio = 1.0 * HALF
    blank = jnp.zeros_like(cond[:1])
    padded = jnp.concatenate([blank, cond, blank])
    face_low = 0.5 * (padded[:-2] + padded[1:-1])
    face_high = 0.5 * (padded[1:-1] + padded[2:])
    below_band = jnp.concatenate([blank, -half_ratio * face_low[1:]])
    above_band = jnp.concatenate([-half_ratio * face_high[:-1], blank])
    main_band = 1.0 + half_ratio * (face_low + face_high)
    return solve_lines(below_band, main_band, above_band, right_side)


def operator(padded):
    field = padded[0]
    cond = padded[1]
    centre = field[1:-1, 1:-1, 1:-1]
    middle = cond[1:-1, 1:-1, 1:-1]
    total = 0.5 * (middle + cond[:-2, 1:-1, 1:-1]) * (field[:-2, 1:-1, 1:-1] - centre)
    total = total + 0.5 * (middle + cond[2:, 1:-1, 1:-1]) * (field[2:, 1:-1, 1:-1] - centre)
    total = total + 0.5 * (middle + cond[1:-1, :-2, 1:-1]) * (field[1:-1, :-2, 1:-1] - centre)
    total = total + 0.5 * (middle + cond[1:-1, 2:, 1:-1]) * (field[1:-1, 2:, 1:-1] - centre)
    total = total + 0.5 * (middle + cond[1:-1, 1:-1, :-2]) * (field[1:-1, 1:-1, :-2] - centre)
    total = total + 0.5 * (middle + cond[1:-1, 1:-1, 2:]) * (field[1:-1, 1:-1, 2:] - centre)
    return total


def padded_pair(ghost_padded):
    return jnp.pad(ghost_padded, ((0, 0), (1, 1), (0, 0), (0, 0)))


def solve_second(pieces):
    values, conds = pieces
    return (line_solve(conds, values), conds)


def per_device(initial_warmth_state, diffusivity_coefficient, heating_supply, known_forcing_vector):
    time_ratio = 2.0 * HALF
    first = line_solve(diffusivity_coefficient, time_ratio * known_forcing_vector)
    second, cond_second = solve_second(
        (
            lax.all_to_all(
                jnp.swapaxes(first, 0, 1), "wide", split_axis=1, concat_axis=0, tiled=True
            ),
            lax.all_to_all(
                jnp.swapaxes(diffusivity_coefficient, 0, 1),
                "wide",
                split_axis=1,
                concat_axis=0,
                tiled=True,
            ),
        )
    )
    third_in, cond_third = (
        lax.all_to_all(second, "narrow", split_axis=0, concat_axis=2, tiled=True),
        lax.all_to_all(cond_second, "narrow", split_axis=0, concat_axis=2, tiled=True),
    )
    y_count, x_count, z_count = third_in.shape
    cond_lines = cond_third.reshape(y_count * x_count, z_count).T
    depthwise_pass = line_solve(cond_lines, third_in.reshape(y_count * x_count, z_count).T)
    third_block = depthwise_pass.T.reshape(y_count, x_count, z_count)
    flipped_array = lax.all_to_all(
        lax.all_to_all(third_block, "narrow", split_axis=2, concat_axis=0, tiled=True),
        "wide",
        split_axis=0,
        concat_axis=1,
        tiled=True,
    )
    advanced_warmth_state = initial_warmth_state + jnp.swapaxes(flipped_array, 0, 1)
    ghost_padded = extended(
        jnp.stack([advanced_warmth_state, diffusivity_coefficient]), (("wide", 2), ("narrow", 3)), 1
    )
    upcoming_forcing_vector = heating_supply + operator(padded_pair(ghost_padded))
    return (advanced_warmth_state, upcoming_forcing_vector)


def solution(mesh):
    placed = (
        P(None, "wide", "narrow"),
        P(None, "wide", "narrow"),
        P(None, "wide", "narrow"),
        P(None, "wide", "narrow"),
    )
    return jax.shard_map(
        per_device,
        mesh=mesh,
        in_specs=placed,
        out_specs=(P(None, "wide", "narrow"), P(None, "wide", "narrow")),
        check_vma=False,
    )
```

profile of v0, /device:TPU:13, one launch (start us, length us, event | category | flops | bytes accessed | tf_op | source)
XLA Modules:
  0.0 147.1 jit_solution(10686847486221317631)
XLA Ops:
  0.6 6.7 %all-to-all-start.1 = ((f32[8,128,128]{2,0,1:T(8,128)}), f32[8,128,128]{2,0,1:T(8,128)S(1)}, u32[]{:S(2)}, u32[]{:S(2)}) async-start(f32[8,128,128]{2,0,1:T(8,128)} %bitcast.159), calls=%async_computation.1 | async-start | bytes 1048576 | tf_op jit(solution)/shard_map/all_to_all | solution.py:95
  7.3 1.7 %multiply_add_fusion.2 = (f32[128,8,128]{2,1,0:T(8,128)S(1)}, f32[128,8,128]{2,1,0:T(8,128)S(1)}, f32[128,8,128]{2,1,0:T(8,128)S(1)}) fusion(f32[128,8,128]{2,1,0:T(8,128)} %param.5), kind=kLoop, calls=%fused_computation.71 | loop fusion | flops 917504 | bytes 2097152 | tf_op jit(solution)/shard_map/add | solution.py:60
  11.1 0.8 copy.415
  12.0 9.0 %all-to-all-done.1 = f32[8,128,128]{2,0,1:T(8,128)S(1)} async-done(((f32[8,128,128]{2,0,1:T(8,128)}), f32[8,128,128]{2,0,1:T(8,128)S(1)}, u32[]{:S(2)}, u32[]{:S(2)}) %all-to-all-start.1) | async-done | bytes 524320 | tf_op jit(solution)/shard_map/all_to_all | solution.py:95
  20.9 5.0 %all-to-all-start = ((f32[8,128,128]{2,0,1:T(8,128)}), f32[8,128,128]{2,0,1:T(8,128)S(1)}, u32[]{:S(2)}, u32[]{:S(2)}) async-start(f32[8,128,128]{2,0,1:T(8,128)} %bitcast.21), calls=%async_computation | async-start | bytes 1048576 | tf_op jit(solution)/shard_map/all_to_all | solution.py:92
  25.9 0.9 copy.418
  26.8 1.6 %multiply_add_fusion.1 = (f32[128,8,128]{2,1,0:T(8,128)S(1)}, f32[128,8,128]{2,1,0:T(8,128)S(1)}, f32[128,8,128]{2,1,0:T(8,128)S(1)}) fusion(f32[128,8,128]{2,1,0:T(8,128)} %bitcast.29), kind=kLoop, calls=%fused_computation.69 | loop fusion | flops 917504 | bytes 2097152 | tf_op jit(solution)/shard_map/add | solution.py:60
  28.7 10.8 %all-to-all-done = f32[8,128,128]{2,0,1:T(8,128)S(1)} async-done(((f32[8,128,128]{2,0,1:T(8,128)}), f32[8,128,128]{2,0,1:T(8,128)S(1)}, u32[]{:S(2)}, u32[]{:S(2)}) %all-to-all-start) | async-done | bytes 524320 | tf_op jit(solution)/shard_map/all_to_all | solution.py:92
  39.5 3.5 %all-to-all-start.3 = ((f32[128,8,128]{2,1,0:T(8,128)}), f32[128,8,128]{2,1,0:T(8,128)S(1)}, u32[]{:S(2)}, u32[]{:S(2)}) async-start(f32[128,8,128]{2,1,0:T(8,128)} %bitcast.29), calls=%async_computation.3 | async-start | bytes 1048576 | tf_op jit(solution)/shard_map/all_to_all | solution.py:106
  44.9 0.8 copy.429
  45.7 5.2 %all-to-all-done.3 = f32[128,8,128]{2,1,0:T(8,128)S(1)} async-done(((f32[128,8,128]{2,1,0:T(8,128)}), f32[128,8,128]{2,1,0:T(8,128)S(1)}, u32[]{:S(2)}, u32[]{:S(2)}) %all-to-all-start.3) | async-done | bytes 524320 | tf_op jit(solution)/shard_map/all_to_all | solution.py:106
  50.9 3.5 %all-to-all-start.2 = ((f32[128,8,128]{2,1,0:T(8,128)}), f32[128,8,128]{2,1,0:T(8,128)S(1)}, u32[]{:S(2)}, u32[]{:S(2)}) async-start(f32[128,8,128]{2,1,0:T(8,128)} %bitcast.51), calls=%async_computation.2 | async-start | bytes 1048576 | tf_op jit(solution)/shard_map/all_to_all | solution.py:105
  55.0 0.3 slice.1131
  55.3 0.3 slice.1123
  56.0 1.4 slice.1130
  57.4 1.4 slice.1119
  58.8 2.6 %all-to-all-done.2 = f32[128,8,128]{2,1,0:T(8,128)S(1)} async-done(((f32[128,8,128]{2,1,0:T(8,128)}), f32[128,8,128]{2,1,0:T(8,128)S(1)}, u32[]{:S(2)}, u32[]{:S(2)}) %all-to-all-start.2) | async-done | bytes 524320 | tf_op jit(solution)/shard_map/all_to_all | solution.py:105
  61.6 0.3 slice.1114
  62.0 1.4 slice.1118
  63.4 0.7 slice.1316
  64.1 0.8 slice.1319
  65.2 1.4 multiply_add_fusion.4
  71.1 0.4 copy.446
  71.5 0.4 reshape.110
  72.1 0.5 copy.448
  72.5 0.7 reshape.112
  73.2 8.5 %all_to_all.102 = f32[2,1,65536]{2,1,0:T(1,128)S(1)} all-to-all(f32[2,1,65536]{2,1,0:T(1,128)S(1)} %reshape.112), channel_id=1, replica_groups=mesh['wide'=16,'narrow'=2] {'narrow'}, dimensions={0} | all-to-all | bytes 1048576 | tf_op jit(solution)/shard_map/all_to_all | solution.py:113
  81.7 0.5 broadcast.303
  82.2 2.3 %reduce = f32[2,65536]{1,0:T(2,128)S(1)} reduce(f32[2,1,65536]{2,1,0:T(1,128)S(1)} %all_to_all.102, f32[]{:T(128)} %broadcast.303), dimensions={1}, to_apply=%all_to_all.88.reduce_sub_computation | reduce | bytes 1048580 | tf_op jit(solution)/shard_map/all_to_all | solution.py:113
  84.5 0.6 reshape.113
  85.1 0.5 copy.449
  85.7 21.1 %all_to_all.103 = f32[128,8,128]{2,1,0:T(8,128)S(1)} all-to-all(f32[128,8,128]{2,1,0:T(8,128)S(1)} %bitcast.188), channel_id=1, replica_groups=mesh['wide'=16,'narrow'=2] {'wide'}, dimensions={0} | all-to-all | bytes 1048576 | tf_op jit(solution)/shard_map/all_to_all | solution.py:112
  106.9 0.3 bitcast_add_fusion
  107.4 3.6 %collective-permute-start = (f32[2,128,1,128]{3,2,1,0:T(1,128)S(1)}, f32[2,128,1,128]{3,2,1,0:T(1,128)S(1)}, u32[]{:S(2)}, u32[]{:S(2)}) collective-permute-start(f32[2,128,1,128]{3,2,1,0:T(1,128)S(1)} %get-tuple-element.31), channel_id=1, source_target_pairs={{0,2},{2,4},{4,6},{6,8},{8,10},{10,12},{12,14},{14,16},{16,18},{18... | collective-permute-start | bytes 393224 | tf_op jit(solution)/shard_map/ppermute | solution.py:17
  111.0 1.9 %collective-permute-start.1 = (f32[2,128,1,128]{3,2,1,0:T(1,128)S(1)}, f32[2,128,1,128]{3,2,1,0:T(1,128)S(1)}, u32[]{:S(2)}, u32[]{:S(2)}) collective-permute-start(f32[2,128,1,128]{3,2,1,0:T(1,128)S(1)} %get-tuple-element.32), channel_id=1, source_target_pairs={{2,0},{4,2},{6,4},{8,6},{10,8},{12,10},{14,12},{16,14},{18,16},{20... | collective-permute-start | bytes 393224 | tf_op jit(solution)/shard_map/ppermute | solution.py:19
  113.0 5.2 %collective-permute-done.1 = f32[2,128,1,128]{3,2,1,0:T(1,128)S(1)} collective-permute-done((f32[2,128,1,128]{3,2,1,0:T(1,128)S(1)}, f32[2,128,1,128]{3,2,1,0:T(1,128)S(1)}, u32[]{:S(2)}, u32[]{:S(2)}) %collective-permute-start.1) | collective-permute-done | bytes 131104 | tf_op jit(solution)/shard_map/ppermute | solution.py:19
  118.2 0.4 pad_maximum_fusion
  118.6 2.0 %fusion.90 = (f32[2,128,10,1]{3,2,1,0:T(8,128)}, f32[2,128,10,1]{3,2,1,0:T(8,128)S(1)}) fusion(f32[2,128,10,128]{3,2,1,0:T(8,128)S(1)} %pad_maximum_fusion), kind=kLoop, calls=%fused_computation.290 | loop fusion | bytes 40960 | tf_op jit(solution)/shard_map/slice | solution.py:14
  120.6 2.2 %copy.453 = f32[2,128,10,1]{1,0,3,2:T(2,128)S(1)} copy(f32[2,128,10,1]{3,2,1,0:T(8,128)} %get-tuple-element.25) | data formatting | bytes 20480 | tf_op jit(solution)/shard_map/slice | solution.py:14
  122.8 2.1 %collective-permute-start.2 = (f32[2,128,10,1]{1,0,3,2:T(2,128)S(1)}, f32[2,128,10,1]{1,0,3,2:T(2,128)S(1)}, u32[]{:S(2)}, u32[]{:S(2)}) collective-permute-start(f32[2,128,10,1]{1,0,3,2:T(2,128)S(1)} %copy.453), channel_id=1, source_target_pairs={{0,1},{2,3},{4,5},{6,7},{8,9},{10,11},{12,13},{14,15},{16,17},{18,... | collective-permute-start | bytes 30728 | tf_op jit(solution)/shard_map/ppermute | solution.py:17
  124.9 0.7 copy.454
  125.6 1.3 collective-permute-start.3
  126.9 0.9 copy.455
  127.9 2.2 %collective-permute-done.3 = f32[2,128,10,1]{1,0,3,2:T(2,128)S(1)} collective-permute-done((f32[2,128,10,1]{1,0,3,2:T(2,128)S(1)}, f32[2,128,10,1]{1,0,3,2:T(2,128)S(1)}, u32[]{:S(2)}, u32[]{:S(2)}) %collective-permute-start.3) | collective-permute-done | bytes 10272 | tf_op jit(solution)/shard_map/ppermute | solution.py:19
  130.0 2.1 %copy.456 = f32[2,128,10,1]{3,2,1,0:T(8,128)} copy(f32[2,128,10,1]{1,0,3,2:T(2,128)S(1)} %collective-permute-done.3) | data formatting | bytes 20480 | tf_op jit(solution)/shard_map/ppermute | solution.py:19
  132.2 5.2 %select_maximum_fusion = f32[2,130,10,130]{3,2,1,0:T(8,128)S(1)} fusion(f32[2,128,10,1]{3,2,1,0:T(8,128)} %copy.456, f32[2,128,10,1]{3,2,1,0:T(8,128)S(1)} %copy.455, f32[2,128,1,128]{3,2,1,0:T(1,128)S(1)} %collective-permute-done.1, f32[2,128,1,128]{3,2,1,0:T(1,128)S(1)} %collective-permute-done, f32[1,128,8,128]{3,2,1,0:T(8,128)S(1)} %bitcast.162, ...), kind=kLoop, calls=%fused_computation.2 | loop fusion | flops 4732000 | bytes 2683200 | tf_op jit(solution)/shard_map/concatenate | solution.py:15
  137.4 1.8 %slice_bitcast_fusion.1 = (f32[130,10,130]{2,1,0:T(8,128)S(1)}, f32[130,10,130]{2,1,0:T(8,128)}) fusion(f32[2,130,10,130]{3,2,1,0:T(8,128)S(1)} %select_maximum_fusion), kind=kLoop, calls=%fused_computation.9 | loop fusion | bytes 2704000 | tf_op jit(solution)/shard_map/squeeze | solution.py:66
  139.2 7.9 %fusion.15 = f32[128,8,128]{2,1,0:T(8,128)} fusion(f32[128,8,128]{2,1,0:T(8,128)S(1)} %copy-done.6, f32[130,10,130]{2,1,0:T(8,128)} %get-tuple-element.24, f32[130,10,130]{2,1,0:T(8,128)S(1)} %get-tuple-element.23), kind=kLoop, calls=%fused_computation.32 | loop fusion | flops 3932160 | bytes 8388608 | tf_op jit(solution)/shard_map/add | solution.py:123
  (307 shorter events, 8.9 us)
Async XLA Ops:
  0.6 8.4 %copy-start.7 = (f32[128,8,128]{2,1,0:T(8,128)S(1)}, f32[128,8,128]{2,1,0:T(8,128)}, u32[]{:S(2)}) copy-start(f32[128,8,128]{2,1,0:T(8,128)} %param.7) | copy-start | bytes 1572868
  0.6 20.3 %all-to-all-start.1 = ((f32[8,128,128]{2,0,1:T(8,128)}), f32[8,128,128]{2,0,1:T(8,128)S(1)}, u32[]{:S(2)}, u32[]{:S(2)}) async-start(f32[8,128,128]{2,0,1:T(8,128)} %bitcast.159), calls=%async_computation.1 | async-start | bytes 1048576 | tf_op jit(solution)/shard_map/all_to_all | solution.py:95
  20.9 18.6 %all-to-all-start = ((f32[8,128,128]{2,0,1:T(8,128)}), f32[8,128,128]{2,0,1:T(8,128)S(1)}, u32[]{:S(2)}, u32[]{:S(2)}) async-start(f32[8,128,128]{2,0,1:T(8,128)} %bitcast.21), calls=%async_computation | async-start | bytes 1048576 | tf_op jit(solution)/shard_map/all_to_all | solution.py:92
  39.5 11.4 %all-to-all-start.3 = ((f32[128,8,128]{2,1,0:T(8,128)}), f32[128,8,128]{2,1,0:T(8,128)S(1)}, u32[]{:S(2)}, u32[]{:S(2)}) async-start(f32[128,8,128]{2,1,0:T(8,128)} %bitcast.29), calls=%async_computation.3 | async-start | bytes 1048576 | tf_op jit(solution)/shard_map/all_to_all | solution.py:106
  50.9 10.5 %all-to-all-start.2 = ((f32[128,8,128]{2,1,0:T(8,128)}), f32[128,8,128]{2,1,0:T(8,128)S(1)}, u32[]{:S(2)}, u32[]{:S(2)}) async-start(f32[128,8,128]{2,1,0:T(8,128)} %bitcast.51), calls=%async_computation.2 | async-start | bytes 1048576 | tf_op jit(solution)/shard_map/all_to_all | solution.py:105
  61.4 3.8 %copy-start.2 = (f32[128,512]{1,0:T(8,128)S(1)}, f32[128,512]{1,0:T(8,128)}, u32[]{:S(2)}) copy-start(f32[128,512]{1,0:T(8,128)} %slice.1130) | copy-start | bytes 786436
  61.4 3.8 %copy-start.3 = (f32[128,512]{1,0:T(8,128)S(1)}, f32[128,512]{1,0:T(8,128)}, u32[]{:S(2)}) copy-start(f32[128,512]{1,0:T(8,128)} %slice.1119) | copy-start | bytes 786436
  63.4 1.9 %copy-start.4 = (f32[128,512]{1,0:T(8,128)S(1)}, f32[128,512]{1,0:T(8,128)}, u32[]{:S(2)}) copy-start(f32[128,512]{1,0:T(8,128)} %slice.1118) | copy-start | bytes 786436
  85.1 21.7 %copy-start.5 = (f32[128,8,128]{2,1,0:T(8,128)S(1)}, f32[128,8,128]{2,1,0:T(8,128)}, u32[]{:S(2)}) copy-start(f32[128,8,128]{2,1,0:T(8,128)} %param.4) | copy-start | bytes 1572868
  85.6 21.6 %copy-start = (f32[128,8,128]{2,1,0:T(8,128)S(1)}, f32[128,8,128]{2,1,0:T(8,128)}, u32[]{:S(2)}) copy-start(f32[128,8,128]{2,1,0:T(8,128)} %param.5) | copy-start | bytes 1572868
  107.2 25.0 %copy-start.1 = (f32[128,8,128]{2,1,0:T(8,128)}, f32[128,8,128]{2,1,0:T(8,128)S(1)}, u32[]{:S(2)}) copy-start(f32[128,8,128]{2,1,0:T(8,128)S(1)} %bitcast_add_fusion) | copy-start | bytes 1572868
  107.4 5.6 %collective-permute-start = (f32[2,128,1,128]{3,2,1,0:T(1,128)S(1)}, f32[2,128,1,128]{3,2,1,0:T(1,128)S(1)}, u32[]{:S(2)}, u32[]{:S(2)}) collective-permute-start(f32[2,128,1,128]{3,2,1,0:T(1,128)S(1)} %get-tuple-element.31), channel_id=1, source_target_pairs={{0,2},{2,4},{4,6},{6,8},{8,10},{10,12},{12,14},{14,16},{16,18},{18... | collective-permute-start | bytes 393224 | tf_op jit(solution)/shard_map/ppermute | solution.py:17
  111.0 7.2 %collective-permute-start.1 = (f32[2,128,1,128]{3,2,1,0:T(1,128)S(1)}, f32[2,128,1,128]{3,2,1,0:T(1,128)S(1)}, u32[]{:S(2)}, u32[]{:S(2)}) collective-permute-start(f32[2,128,1,128]{3,2,1,0:T(1,128)S(1)} %get-tuple-element.32), channel_id=1, source_target_pairs={{2,0},{4,2},{6,4},{8,6},{10,8},{12,10},{14,12},{16,14},{18,16},{20... | collective-permute-start | bytes 393224 | tf_op jit(solution)/shard_map/ppermute | solution.py:19
  122.8 4.1 %collective-permute-start.2 = (f32[2,128,10,1]{1,0,3,2:T(2,128)S(1)}, f32[2,128,10,1]{1,0,3,2:T(2,128)S(1)}, u32[]{:S(2)}, u32[]{:S(2)}) collective-permute-start(f32[2,128,10,1]{1,0,3,2:T(2,128)S(1)} %copy.453), channel_id=1, source_target_pairs={{0,1},{2,3},{4,5},{6,7},{8,9},{10,11},{12,13},{14,15},{16,17},{18,... | collective-permute-start | bytes 30728 | tf_op jit(solution)/shard_map/ppermute | solution.py:17
  125.6 4.4 %collective-permute-start.3 = (f32[2,128,10,1]{1,0,3,2:T(2,128)S(1)}, f32[2,128,10,1]{1,0,3,2:T(2,128)S(1)}, u32[]{:S(2)}, u32[]{:S(2)}) collective-permute-start(f32[2,128,10,1]{1,0,3,2:T(2,128)S(1)} %copy.454), channel_id=1, source_target_pairs={{1,0},{3,2},{5,4},{7,6},{9,8},{11,10},{13,12},{15,14},{17,16},{19,... | collective-permute-start | bytes 30728 | tf_op jit(solution)/shard_map/ppermute | solution.py:19
  137.4 1.8 %copy-start.6 = (f32[128,8,128]{2,1,0:T(8,128)S(1)}, f32[128,8,128]{2,1,0:T(8,128)}, u32[]{:S(2)}) copy-start(f32[128,8,128]{2,1,0:T(8,128)} %param.6) | copy-start | bytes 1572868
where the time goes:
time: 148 us; the launch traced here: 147 us
  waiting for transfers between devices  35 us (24%)
  blocking collectives  29.6 us (20%)
  local copies, waits for them, and re-layouts  27.9 us (19%)
  starting transfers between devices  27.6 us (19%)
  other arithmetic  24.2 us (16%)
  between operations  2.76 us (2%)
    all_to_all x1, blocking collectives, per_device(): lax.all_to_all(lax.all_to_all(third_block, 'narrow', split_axis=2, concat...  21.1 us
    all_to_all x1, waiting for transfers between devices, per_device(): lax.all_to_all(jnp.swapaxes(first, 0, 1), 'wide', split_axis=1, concat_ax...  10.8 us
    all_to_all x1, waiting for transfers between devices, per_device(): lax.all_to_all(jnp.swapaxes(diffusivity_coefficient, 0, 1), 'wide', split...  8.98 us
    all_to_all x1, blocking collectives, per_device(): lax.all_to_all(third_block, 'narrow', split_axis=2, concat_axis=0, tiled=...  8.48 us
    add x1, other arithmetic, per_device(): heating_supply + operator(padded_pair(ghost_padded))  7.86 us
    ppermute x2, waiting for transfers between devices, extended(): lax.ppermute(head, axis, [((i + 1) % count, i) for i in range(ends)])  7.41 us
    all_to_all x1, starting transfers between devices, per_device(): lax.all_to_all(jnp.swapaxes(diffusivity_coefficient, 0, 1), 'wide', split...  6.7 us
    ppermute x2, starting transfers between devices, extended(): lax.ppermute(tail, axis, [(i, (i + 1) % count) for i in range(ends)])  5.73 us
  transfers between devices with their start and end apart: 8, of which 6 were waited for; matrix products, arithmetic and copies ran while one was open for 10% of the time, Pallas kernels for 0%

commit v1 on v0

--- a/solution.py
+++ b/solution.py
@@ -4,6 +4,22 @@
 from jax.sharding import PartitionSpec as P
 
 HALF = 256
+
+
+def tasks_advance(inputs, array_axis, target):
+    b_now = inputs.shape
+    front = inputs.reshape(
+        *b_now[:array_axis], target, b_now[array_axis] // target, *b_now[array_axis + 1 :]
+    )
+    return jnp.moveaxis(front, array_axis, 0)
+
+
+def report_the_leaf(body, row_dim):
+    body = jnp.moveaxis(body, 0, row_dim)
+    tile_out = body.shape
+    return body.reshape(
+        *tile_out[:row_dim], tile_out[row_dim] * tile_out[row_dim + 1], *tile_out[row_dim + 2 :]
+    )
 
 
 def extended(cells, sides, width):
@@ -87,11 +103,26 @@
 def per_device(initial_warmth_state, diffusivity_coefficient, heating_supply, known_forcing_vector):
     time_ratio = 2.0 * HALF
     first = line_solve(diffusivity_coefficient, time_ratio * known_forcing_vector)
+
+    def shape_slot(slab_in, mesh_dim, mat, vector):
+        current_value = lax.axis_size(mesh_dim)
+        small, d_next = (current_value, lax.axis_index(mesh_dim))
+        oldest = tasks_advance(slab_in, mat, small)
+        ix = 1
+        sheets = [oldest[d_next]]
+        while ix < small:
+            u1 = oldest[d_next ^ ix]
+            sheets.append(
+                lax.ppermute(u1, axis_name=mesh_dim, perm=[(ii, ii ^ ix) for ii in range(small)])
+            )
+            ix += 1
+        parts_out = jnp.stack(sheets, 0)
+        oldest = parts_out[d_next ^ jnp.arange(small)]
+        return report_the_leaf(oldest, vector)
+
     second, cond_second = solve_second(
         (
-            lax.all_to_all(
-                jnp.swapaxes(first, 0, 1), "wide", split_axis=1, concat_axis=0, tiled=True
-            ),
+            shape_slot(jnp.swapaxes(first, 0, 1), "wide", 1, 0),
             lax.all_to_all(
                 jnp.swapaxes(diffusivity_coefficient, 0, 1),
                 "wide",

time: 148 us -> 147 us (level)
  waiting for transfers between devices: 35 us -> 17.7 us
  starting transfers between devices: 27.6 us -> 40.3 us
  blocking collectives: 29.6 us -> 34.7 us
    ppermute x0 -> x15, starting transfers between devices: none -> 17.5 us  [shape_slot(): lax.ppermute(u1, axis_name=mesh_dim, perm=[(ii, ii ^ ix) for ii in range(...]
    all_to_all x1 -> x0, waiting for transfers between devices: 10.8 us -> none  [per_device(): lax.all_to_all(jnp.swapaxes(first, 0, 1), 'wide', split_axis=1, concat_ax...]
    all_to_all x1, waiting for transfers between devices: 8.98 us -> 0.01 us  [per_device(): lax.all_to_all(jnp.swapaxes(diffusivity_coefficient, 0, 1), 'wide', split...]
    all_to_all x1, blocking collectives: 21.1 us -> 26.4 us  [per_device(): lax.all_to_all(lax.all_to_all(third_block, 'narrow', split_axis=2, concat...]
    all_to_all x1 -> x0, starting transfers between devices: 4.98 us -> none  [per_device(): lax.all_to_all(jnp.swapaxes(first, 0, 1), 'wide', split_axis=1, concat_ax...]
    ppermute x0 -> x15, waiting for transfers between devices: none -> 3.8 us  [shape_slot(): lax.ppermute(u1, axis_name=mesh_dim, perm=[(ii, ii ^ ix) for ii in range(...]
    all_to_all x1, waiting for transfers between devices: 5.18 us -> 2.45 us  [per_device(): lax.all_to_all(cond_second, 'narrow', split_axis=0, concat_axis=2, tiled=...]
    all_to_all x1, waiting for transfers between devices: 2.55 us -> 4.21 us  [per_device(): lax.all_to_all(second, 'narrow', split_axis=0, concat_axis=2, tiled=True)]
  transfers between devices with their start and end apart: 8 -> 22, of which waited for: 6 -> 8; matrix products, arithmetic and copies ran while one was open for 10% -> 8% of each run, Pallas kernels for 0% -> 0%
where the time goes in v1:
time: 147 us; the launch traced here: 146 us
  starting transfers between devices  40.3 us (27%)
  blocking collectives  34.7 us (24%)
  local copies, waits for them, and re-layouts  26.6 us (18%)
  other arithmetic  24.1 us (16%)
  waiting for transfers between devices  17.7 us (12%)
  between operations  3 us (2%)
    all_to_all x1, blocking collectives, per_device(): lax.all_to_all(lax.all_to_all(third_block, 'narrow', split_axis=2, concat...  26.4 us
    ppermute x15, starting transfers between devices, shape_slot(): lax.ppermute(u1, axis_name=mesh_dim, perm=[(ii, ii ^ ix) for ii in range(...  17.5 us
    all_to_all x1, blocking collectives, per_device(): lax.all_to_all(third_block, 'narrow', split_axis=2, concat_axis=0, tiled=...  8.27 us
    add x1, other arithmetic, per_device(): heating_supply + operator(padded_pair(ghost_padded))  7.84 us
    ppermute x2, waiting for transfers between devices, extended(): lax.ppermute(head, axis, [((i + 1) % count, i) for i in range(ends)])  7.19 us
    all_to_all x1, starting transfers between devices, per_device(): lax.all_to_all(jnp.swapaxes(diffusivity_coefficient, 0, 1), 'wide', split...  6.7 us
    concatenate x2, other arithmetic, extended(): jnp.concatenate([lax.ppermute(tail, axis, [(i, (i + 1) % count) for i in...  5.6 us
    ppermute x2, starting transfers between devices, extended(): lax.ppermute(tail, axis, [(i, (i + 1) % count) for i in range(ends)])  5.55 us
  transfers between devices with their start and end apart: 22, of which 8 were waited for; matrix products, arithmetic and copies ran while one was open for 8% of the time, Pallas kernels for 0%

profile of v1, /device:TPU:13, one launch (start us, length us, event | category | flops | bytes accessed | tf_op | source)
XLA Modules:
  0.0 146.4 jit_solution(4937889904046270121)
XLA Ops:
  0.6 6.7 %all-to-all-start = ((f32[8,128,128]{2,0,1:T(8,128)}), f32[8,128,128]{2,0,1:T(8,128)S(1)}, u32[]{:S(2)}, u32[]{:S(2)}) async-start(f32[8,128,128]{2,0,1:T(8,128)} %bitcast.239), calls=%async_computation | async-start | bytes 1048576 | tf_op jit(solution)/shard_map/all_to_all | solution.py:126
  7.3 1.6 %multiply_add_fusion.2 = (f32[128,8,128]{2,1,0:T(8,128)S(1)}, f32[128,8,128]{2,1,0:T(8,128)S(1)}, f32[128,8,128]{2,1,0:T(8,128)S(1)}) fusion(f32[128,8,128]{2,1,0:T(8,128)} %param.5), kind=kLoop, calls=%fused_computation.72 | loop fusion | flops 917504 | bytes 2097152 | tf_op jit(solution)/shard_map/add | solution.py:76
  12.0 1.6 %collective-permute-start.2 = (f32[8,8,128]{2,1,0:T(8,128)S(1)}, f32[8,8,128]{2,1,0:T(8,128)S(1)}, u32[]{:S(2)}, u32[]{:S(2)}) collective-permute-start(f32[8,8,128]{2,1,0:T(8,128)S(1)} %bitcast.311), channel_id=1, source_target_pairs={{0,6},{2,4},{4,2},{6,0},{8,14},{10,12},{12,10},{14,8},{16,22},{18,... | collective-permute-start | bytes 98312 | tf_op jit(solution)/shard_map/ppermute | solution.py:116
  14.0 1.5 %collective-permute-start.4 = (f32[8,8,128]{2,1,0:T(8,128)S(1)}, f32[8,8,128]{2,1,0:T(8,128)S(1)}, u32[]{:S(2)}, u32[]{:S(2)}) collective-permute-start(f32[8,8,128]{2,1,0:T(8,128)S(1)} %bitcast.308), channel_id=1, source_target_pairs={{0,10},{2,8},{4,14},{6,12},{8,2},{10,0},{12,6},{14,4},{16,26},{18,... | collective-permute-start | bytes 98312 | tf_op jit(solution)/shard_map/ppermute | solution.py:116
  15.8 2.6 %collective-permute-start.6 = (f32[8,8,128]{2,1,0:T(8,128)S(1)}, f32[8,8,128]{2,1,0:T(8,128)S(1)}, u32[]{:S(2)}, u32[]{:S(2)}) collective-permute-start(f32[8,8,128]{2,1,0:T(8,128)S(1)} %bitcast.310), channel_id=1, source_target_pairs={{0,14},{2,12},{4,10},{6,8},{8,6},{10,4},{12,2},{14,0},{16,30},{18,... | collective-permute-start | bytes 98312 | tf_op jit(solution)/shard_map/ppermute | solution.py:116
  18.4 2.1 %collective-permute-start.7 = (f32[8,8,128]{2,1,0:T(8,128)S(1)}, f32[8,8,128]{2,1,0:T(8,128)S(1)}, u32[]{:S(2)}, u32[]{:S(2)}) collective-permute-start(f32[8,8,128]{2,1,0:T(8,128)S(1)} %bitcast.307), channel_id=1, source_target_pairs={{0,16},{2,18},{4,20},{6,22},{8,24},{10,26},{12,28},{14,30},{16,0},... | collective-permute-start | bytes 98312 | tf_op jit(solution)/shard_map/ppermute | solution.py:116
  20.5 0.5 collective-permute-start.8
  21.0 2.1 %collective-permute-start.9 = (f32[8,8,128]{2,1,0:T(8,128)S(1)}, f32[8,8,128]{2,1,0:T(8,128)S(1)}, u32[]{:S(2)}, u32[]{:S(2)}) collective-permute-start(f32[8,8,128]{2,1,0:T(8,128)S(1)} %bitcast.305), channel_id=1, source_target_pairs={{0,20},{2,22},{4,16},{6,18},{8,28},{10,30},{12,24},{14,26},{16,4},... | collective-permute-start | bytes 98312 | tf_op jit(solution)/shard_map/ppermute | solution.py:116
  23.1 1.5 %collective-permute-start.10 = (f32[8,8,128]{2,1,0:T(8,128)S(1)}, f32[8,8,128]{2,1,0:T(8,128)S(1)}, u32[]{:S(2)}, u32[]{:S(2)}) collective-permute-start(f32[8,8,128]{2,1,0:T(8,128)S(1)} %bitcast.304), channel_id=1, source_target_pairs={{0,22},{2,20},{4,18},{6,16},{8,30},{10,28},{12,26},{14,24},{16,6},... | collective-permute-start | bytes 98312 | tf_op jit(solution)/shard_map/ppermute | solution.py:116
  24.7 1.2 collective-permute-start.11
  25.8 0.5 collective-permute-start.12
  26.4 1.2 collective-permute-start.13
  27.6 1.5 %collective-permute-start.14 = (f32[8,8,128]{2,1,0:T(8,128)S(1)}, f32[8,8,128]{2,1,0:T(8,128)S(1)}, u32[]{:S(2)}, u32[]{:S(2)}) collective-permute-start(f32[8,8,128]{2,1,0:T(8,128)S(1)} %bitcast.300), channel_id=1, source_target_pairs={{0,30},{2,28},{4,26},{6,24},{8,22},{10,20},{12,18},{14,16},{16,14}... | collective-permute-start | bytes 98312 | tf_op jit(solution)/shard_map/ppermute | solution.py:116
  29.3 1.2 collective-permute-done.12
  31.0 1.8 %collective-permute-done.14 = f32[8,8,128]{2,1,0:T(8,128)S(1)} collective-permute-done((f32[8,8,128]{2,1,0:T(8,128)S(1)}, f32[8,8,128]{2,1,0:T(8,128)S(1)}, u32[]{:S(2)}, u32[]{:S(2)}) %collective-permute-start.14) | collective-permute-done | bytes 32800 | tf_op jit(solution)/shard_map/ppermute | solution.py:116
  32.9 0.6 gather_fusion
  33.5 0.9 copy.516
  34.4 3.5 %all-to-all-start.2 = ((f32[128,8,128]{2,1,0:T(8,128)}), f32[128,8,128]{2,1,0:T(8,128)S(1)}, u32[]{:S(2)}, u32[]{:S(2)}) async-start(f32[128,8,128]{2,1,0:T(8,128)} %bitcast.59), calls=%async_computation.2 | async-start | bytes 1048576 | tf_op jit(solution)/shard_map/all_to_all | solution.py:137
  37.9 1.6 %multiply_add_fusion.1 = (f32[128,8,128]{2,1,0:T(8,128)S(1)}, f32[128,8,128]{2,1,0:T(8,128)S(1)}, f32[128,8,128]{2,1,0:T(8,128)S(1)}) fusion(f32[128,8,128]{2,1,0:T(8,128)} %bitcast.59), kind=kLoop, calls=%fused_computation.70 | loop fusion | flops 917504 | bytes 2097152 | tf_op jit(solution)/shard_map/add | solution.py:76
  39.8 0.8 slice-done
  42.3 0.8 copy.527
  43.1 2.4 %all-to-all-done.2 = f32[128,8,128]{2,1,0:T(8,128)S(1)} async-done(((f32[128,8,128]{2,1,0:T(8,128)}), f32[128,8,128]{2,1,0:T(8,128)S(1)}, u32[]{:S(2)}, u32[]{:S(2)}) %all-to-all-start.2) | async-done | bytes 524320 | tf_op jit(solution)/shard_map/all_to_all | solution.py:137
  45.6 3.7 %all-to-all-start.1 = ((f32[128,8,128]{2,1,0:T(8,128)}), f32[128,8,128]{2,1,0:T(8,128)S(1)}, u32[]{:S(2)}, u32[]{:S(2)}) async-start(f32[128,8,128]{2,1,0:T(8,128)} %bitcast.81), calls=%async_computation.1 | async-start | bytes 1048576 | tf_op jit(solution)/shard_map/all_to_all | solution.py:136
  51.6 4.2 %all-to-all-done.1 = f32[128,8,128]{2,1,0:T(8,128)S(1)} async-done(((f32[128,8,128]{2,1,0:T(8,128)}), f32[128,8,128]{2,1,0:T(8,128)S(1)}, u32[]{:S(2)}, u32[]{:S(2)}) %all-to-all-start.1) | async-done | bytes 524320 | tf_op jit(solution)/shard_map/all_to_all | solution.py:136
  56.4 1.4 slice.1118
  57.8 0.7 slice.1318
  58.6 0.7 slice.1321
  59.7 1.4 multiply_add_fusion.4
  67.0 0.7 reshape.175
  67.6 8.3 %all_to_all.84 = f32[2,1,65536]{2,1,0:T(1,128)S(1)} all-to-all(f32[2,1,65536]{2,1,0:T(1,128)S(1)} %reshape.175), channel_id=1, replica_groups=mesh['wide'=16,'narrow'=2] {'narrow'}, dimensions={0} | all-to-all | bytes 1048576 | tf_op jit(solution)/shard_map/all_to_all | solution.py:144
  75.9 0.5 broadcast.338
  76.4 2.3 %reduce = f32[2,65536]{1,0:T(2,128)S(1)} reduce(f32[2,1,65536]{2,1,0:T(1,128)S(1)} %all_to_all.84, f32[]{:T(128)} %broadcast.338), dimensions={1}, to_apply=%all_to_all.71.reduce_sub_computation | reduce | bytes 1048580 | tf_op jit(solution)/shard_map/all_to_all | solution.py:144
  78.7 0.6 reshape.176
  79.9 26.4 %all_to_all.85 = f32[128,8,128]{2,1,0:T(8,128)S(1)} all-to-all(f32[128,8,128]{2,1,0:T(8,128)S(1)} %bitcast.268), channel_id=1, replica_groups=mesh['wide'=16,'narrow'=2] {'wide'}, dimensions={0} | all-to-all | bytes 1048576 | tf_op jit(solution)/shard_map/all_to_all | solution.py:143
  106.9 3.6 %collective-permute-start.15 = (f32[2,128,1,128]{3,2,1,0:T(1,128)S(1)}, f32[2,128,1,128]{3,2,1,0:T(1,128)S(1)}, u32[]{:S(2)}, u32[]{:S(2)}) collective-permute-start(f32[2,128,1,128]{3,2,1,0:T(1,128)S(1)} %get-tuple-element.31), channel_id=1, source_target_pairs={{0,2},{2,4},{4,6},{6,8},{8,10},{10,12},{12,14},{14,16},{16,18},{18... | collective-permute-start | bytes 393224 | tf_op jit(solution)/shard_map/ppermute | solution.py:33
  110.5 2.1 %collective-permute-start.16 = (f32[2,128,1,128]{3,2,1,0:T(1,128)S(1)}, f32[2,128,1,128]{3,2,1,0:T(1,128)S(1)}, u32[]{:S(2)}, u32[]{:S(2)}) collective-permute-start(f32[2,128,1,128]{3,2,1,0:T(1,128)S(1)} %get-tuple-element.32), channel_id=1, source_target_pairs={{2,0},{4,2},{6,4},{8,6},{10,8},{12,10},{14,12},{16,14},{18,16},{20... | collective-permute-start | bytes 393224 | tf_op jit(solution)/shard_map/ppermute | solution.py:35
  112.7 5.0 %collective-permute-done.16 = f32[2,128,1,128]{3,2,1,0:T(1,128)S(1)} collective-permute-done((f32[2,128,1,128]{3,2,1,0:T(1,128)S(1)}, f32[2,128,1,128]{3,2,1,0:T(1,128)S(1)}, u32[]{:S(2)}, u32[]{:S(2)}) %collective-permute-start.16) | collective-permute-done | bytes 131104 | tf_op jit(solution)/shard_map/ppermute | solution.py:35
  118.1 2.0 %fusion.91 = (f32[2,128,10,1]{3,2,1,0:T(8,128)}, f32[2,128,10,1]{3,2,1,0:T(8,128)S(1)}) fusion(f32[2,128,10,128]{3,2,1,0:T(8,128)S(1)} %pad_maximum_fusion), kind=kLoop, calls=%fused_computation.342 | loop fusion | bytes 40960 | tf_op jit(solution)/shard_map/slice | solution.py:30
  120.1 2.2 %copy.551 = f32[2,128,10,1]{1,0,3,2:T(2,128)S(1)} copy(f32[2,128,10,1]{3,2,1,0:T(8,128)} %get-tuple-element.25) | data formatting | bytes 20480 | tf_op jit(solution)/shard_map/slice | solution.py:30
  122.3 1.9 %collective-permute-start.17 = (f32[2,128,10,1]{1,0,3,2:T(2,128)S(1)}, f32[2,128,10,1]{1,0,3,2:T(2,128)S(1)}, u32[]{:S(2)}, u32[]{:S(2)}) collective-permute-start(f32[2,128,10,1]{1,0,3,2:T(2,128)S(1)} %copy.551), channel_id=1, source_target_pairs={{0,1},{2,3},{4,5},{6,7},{8,9},{10,11},{12,13},{14,15},{16,17},{18,... | collective-permute-start | bytes 30728 | tf_op jit(solution)/shard_map/ppermute | solution.py:33
  124.2 0.7 copy.552
  125.0 1.3 collective-permute-start.18
  126.3 0.9 copy.553
  127.2 2.2 %collective-permute-done.18 = f32[2,128,10,1]{1,0,3,2:T(2,128)S(1)} collective-permute-done((f32[2,128,10,1]{1,0,3,2:T(2,128)S(1)}, f32[2,128,10,1]{1,0,3,2:T(2,128)S(1)}, u32[]{:S(2)}, u32[]{:S(2)}) %collective-permute-start.18) | collective-permute-done | bytes 10272 | tf_op jit(solution)/shard_map/ppermute | solution.py:35
  129.4 2.1 %copy.554 = f32[2,128,10,1]{3,2,1,0:T(8,128)} copy(f32[2,128,10,1]{1,0,3,2:T(2,128)S(1)} %collective-permute-done.18) | data formatting | bytes 20480 | tf_op jit(solution)/shard_map/ppermute | solution.py:35
  131.5 5.2 %select_maximum_fusion = f32[2,130,10,130]{3,2,1,0:T(8,128)S(1)} fusion(f32[2,128,10,1]{3,2,1,0:T(8,128)} %copy.554, f32[2,128,10,1]{3,2,1,0:T(8,128)S(1)} %copy.553, f32[2,128,1,128]{3,2,1,0:T(1,128)S(1)} %collective-permute-done.16, f32[2,128,1,128]{3,2,1,0:T(1,128)S(1)} %collective-permute-done.15, f32[1,128,8,128]{3,2,1,0:T(8,128)S(1)} %bitcast.242, ...), kind=kLoop, calls=%fused_computation.3 | loop fusion | flops 4732000 | bytes 2683200 | tf_op jit(solution)/shard_map/concatenate | solution.py:31
  136.7 1.8 %slice_bitcast_fusion.1 = (f32[130,10,130]{2,1,0:T(8,128)S(1)}, f32[130,10,130]{2,1,0:T(8,128)}) fusion(f32[2,130,10,130]{3,2,1,0:T(8,128)S(1)} %select_maximum_fusion), kind=kLoop, calls=%fused_computation.10 | loop fusion | bytes 2704000 | tf_op jit(solution)/shard_map/squeeze | solution.py:82
  138.6 7.8 %fusion.15 = f32[128,8,128]{2,1,0:T(8,128)} fusion(f32[128,8,128]{2,1,0:T(8,128)S(1)} %copy-done.5, f32[130,10,130]{2,1,0:T(8,128)} %get-tuple-element.24, f32[130,10,130]{2,1,0:T(8,128)S(1)} %get-tuple-element.23), kind=kLoop, calls=%fused_computation.33 | loop fusion | flops 3932160 | bytes 8388608 | tf_op jit(solution)/shard_map/add | solution.py:154
  (368 shorter events, 15.1 us)
Async XLA Ops:
  0.6 8.3 %copy-start.6 = (f32[128,8,128]{2,1,0:T(8,128)S(1)}, f32[128,8,128]{2,1,0:T(8,128)}, u32[]{:S(2)}) copy-start(f32[128,8,128]{2,1,0:T(8,128)} %param.7) | copy-start | bytes 1572868
  0.6 32.9 %all-to-all-start = ((f32[8,128,128]{2,0,1:T(8,128)}), f32[8,128,128]{2,0,1:T(8,128)S(1)}, u32[]{:S(2)}, u32[]{:S(2)}) async-start(f32[8,128,128]{2,0,1:T(8,128)} %bitcast.239), calls=%async_computation | async-start | bytes 1048576 | tf_op jit(solution)/shard_map/all_to_all | solution.py:126
  11.3 4.4 %collective-permute-start = (f32[8,8,128]{2,1,0:T(8,128)S(1)}, f32[8,8,128]{2,1,0:T(8,128)S(1)}, u32[]{:S(2)}, u32[]{:S(2)}) collective-permute-start(f32[8,8,128]{2,1,0:T(8,128)S(1)} %bitcast.313), channel_id=1, source_target_pairs={{0,2},{2,0},{4,6},{6,4},{8,10},{10,8},{12,14},{14,12},{16,18},{18,... | collective-permute-start | bytes 98312 | tf_op jit(solution)/shard_map/ppermute | solution.py:116
  11.7 4.1 %collective-permute-start.1 = (f32[8,8,128]{2,1,0:T(8,128)S(1)}, f32[8,8,128]{2,1,0:T(8,128)S(1)}, u32[]{:S(2)}, u32[]{:S(2)}) collective-permute-start(f32[8,8,128]{2,1,0:T(8,128)S(1)} %bitcast.312), channel_id=1, source_target_pairs={{0,4},{2,6},{4,0},{6,2},{8,12},{10,14},{12,8},{14,10},{16,20},{18,... | collective-permute-start | bytes 98312 | tf_op jit(solution)/shard_map/ppermute | solution.py:116
  12.0 6.4 %collective-permute-start.2 = (f32[8,8,128]{2,1,0:T(8,128)S(1)}, f32[8,8,128]{2,1,0:T(8,128)S(1)}, u32[]{:S(2)}, u32[]{:S(2)}) collective-permute-start(f32[8,8,128]{2,1,0:T(8,128)S(1)} %bitcast.311), channel_id=1, source_target_pairs={{0,6},{2,4},{4,2},{6,0},{8,14},{10,12},{12,10},{14,8},{16,22},{18,... | collective-permute-start | bytes 98312 | tf_op jit(solution)/shard_map/ppermute | solution.py:116
  13.6 6.9 %collective-permute-start.3 = (f32[8,8,128]{2,1,0:T(8,128)S(1)}, f32[8,8,128]{2,1,0:T(8,128)S(1)}, u32[]{:S(2)}, u32[]{:S(2)}) collective-permute-start(f32[8,8,128]{2,1,0:T(8,128)S(1)} %bitcast.309), channel_id=1, source_target_pairs={{0,8},{2,10},{4,12},{6,14},{8,0},{10,2},{12,4},{14,6},{16,24},{18,... | collective-permute-start | bytes 98312 | tf_op jit(solution)/shard_map/ppermute | solution.py:116
  14.0 7.1 %collective-permute-start.4 = (f32[8,8,128]{2,1,0:T(8,128)S(1)}, f32[8,8,128]{2,1,0:T(8,128)S(1)}, u32[]{:S(2)}, u32[]{:S(2)}) collective-permute-start(f32[8,8,128]{2,1,0:T(8,128)S(1)} %bitcast.308), channel_id=1, source_target_pairs={{0,10},{2,8},{4,14},{6,12},{8,2},{10,0},{12,6},{14,4},{16,26},{18,... | collective-permute-start | bytes 98312 | tf_op jit(solution)/shard_map/ppermute | solution.py:116
  15.7 7.5 %collective-permute-start.5 = (f32[8,8,128]{2,1,0:T(8,128)S(1)}, f32[8,8,128]{2,1,0:T(8,128)S(1)}, u32[]{:S(2)}, u32[]{:S(2)}) collective-permute-start(f32[8,8,128]{2,1,0:T(8,128)S(1)} %bitcast.314), channel_id=1, source_target_pairs={{0,12},{2,14},{4,8},{6,10},{8,4},{10,6},{12,0},{14,2},{16,28},{18,... | collective-permute-start | bytes 98312 | tf_op jit(solution)/shard_map/ppermute | solution.py:116
  15.8 8.9 %collective-permute-start.6 = (f32[8,8,128]{2,1,0:T(8,128)S(1)}, f32[8,8,128]{2,1,0:T(8,128)S(1)}, u32[]{:S(2)}, u32[]{:S(2)}) collective-permute-start(f32[8,8,128]{2,1,0:T(8,128)S(1)} %bitcast.310), channel_id=1, source_target_pairs={{0,14},{2,12},{4,10},{6,8},{8,6},{10,4},{12,2},{14,0},{16,30},{18,... | collective-permute-start | bytes 98312 | tf_op jit(solution)/shard_map/ppermute | solution.py:116
  18.4 7.4 %collective-permute-start.7 = (f32[8,8,128]{2,1,0:T(8,128)S(1)}, f32[8,8,128]{2,1,0:T(8,128)S(1)}, u32[]{:S(2)}, u32[]{:S(2)}) collective-permute-start(f32[8,8,128]{2,1,0:T(8,128)S(1)} %bitcast.307), channel_id=1, source_target_pairs={{0,16},{2,18},{4,20},{6,22},{8,24},{10,26},{12,28},{14,30},{16,0},... | collective-permute-start | bytes 98312 | tf_op jit(solution)/shard_map/ppermute | solution.py:116
  20.5 5.8 %collective-permute-start.8 = (f32[8,8,128]{2,1,0:T(8,128)S(1)}, f32[8,8,128]{2,1,0:T(8,128)S(1)}, u32[]{:S(2)}, u32[]{:S(2)}) collective-permute-start(f32[8,8,128]{2,1,0:T(8,128)S(1)} %bitcast.306), channel_id=1, source_target_pairs={{0,18},{2,16},{4,22},{6,20},{8,26},{10,24},{12,30},{14,28},{16,2},... | collective-permute-start | bytes 98312 | tf_op jit(solution)/shard_map/ppermute | solution.py:116
  21.0 6.5 %collective-permute-start.9 = (f32[8,8,128]{2,1,0:T(8,128)S(1)}, f32[8,8,128]{2,1,0:T(8,128)S(1)}, u32[]{:S(2)}, u32[]{:S(2)}) collective-permute-start(f32[8,8,128]{2,1,0:T(8,128)S(1)} %bitcast.305), channel_id=1, source_target_pairs={{0,20},{2,22},{4,16},{6,18},{8,28},{10,30},{12,24},{14,26},{16,4},... | collective-permute-start | bytes 98312 | tf_op jit(solution)/shard_map/ppermute | solution.py:116
  23.1 5.9 %collective-permute-start.10 = (f32[8,8,128]{2,1,0:T(8,128)S(1)}, f32[8,8,128]{2,1,0:T(8,128)S(1)}, u32[]{:S(2)}, u32[]{:S(2)}) collective-permute-start(f32[8,8,128]{2,1,0:T(8,128)S(1)} %bitcast.304), channel_id=1, source_target_pairs={{0,22},{2,20},{4,18},{6,16},{8,30},{10,28},{12,26},{14,24},{16,6},... | collective-permute-start | bytes 98312 | tf_op jit(solution)/shard_map/ppermute | solution.py:116
  24.7 4.6 %collective-permute-start.11 = (f32[8,8,128]{2,1,0:T(8,128)S(1)}, f32[8,8,128]{2,1,0:T(8,128)S(1)}, u32[]{:S(2)}, u32[]{:S(2)}) collective-permute-start(f32[8,8,128]{2,1,0:T(8,128)S(1)} %bitcast.303), channel_id=1, source_target_pairs={{0,24},{2,26},{4,28},{6,30},{8,16},{10,18},{12,20},{14,22},{16,8},... | collective-permute-start | bytes 98312 | tf_op jit(solution)/shard_map/ppermute | solution.py:116
  25.8 4.7 %collective-permute-start.12 = (f32[8,8,128]{2,1,0:T(8,128)S(1)}, f32[8,8,128]{2,1,0:T(8,128)S(1)}, u32[]{:S(2)}, u32[]{:S(2)}) collective-permute-start(f32[8,8,128]{2,1,0:T(8,128)S(1)} %bitcast.302), channel_id=1, source_target_pairs={{0,26},{2,24},{4,30},{6,28},{8,18},{10,16},{12,22},{14,20},{16,10}... | collective-permute-start | bytes 98312 | tf_op jit(solution)/shard_map/ppermute | solution.py:116
  26.4 4.7 %collective-permute-start.13 = (f32[8,8,128]{2,1,0:T(8,128)S(1)}, f32[8,8,128]{2,1,0:T(8,128)S(1)}, u32[]{:S(2)}, u32[]{:S(2)}) collective-permute-start(f32[8,8,128]{2,1,0:T(8,128)S(1)} %bitcast.301), channel_id=1, source_target_pairs={{0,28},{2,30},{4,24},{6,26},{8,20},{10,22},{12,16},{14,18},{16,12}... | collective-permute-start | bytes 98312 | tf_op jit(solution)/shard_map/ppermute | solution.py:116
  27.6 5.3 %collective-permute-start.14 = (f32[8,8,128]{2,1,0:T(8,128)S(1)}, f32[8,8,128]{2,1,0:T(8,128)S(1)}, u32[]{:S(2)}, u32[]{:S(2)}) collective-permute-start(f32[8,8,128]{2,1,0:T(8,128)S(1)} %bitcast.300), channel_id=1, source_target_pairs={{0,30},{2,28},{4,26},{6,24},{8,22},{10,20},{12,18},{14,16},{16,14}... | collective-permute-start | bytes 98312 | tf_op jit(solution)/shard_map/ppermute | solution.py:116
  33.5 6.1 %copy-start.3 = (f32[64,8,128]{2,1,0:T(8,128)}, f32[64,8,128]{2,1,0:T(8,128)S(1)}, u32[]{:S(2)}) copy-start(f32[64,8,128]{2,1,0:T(8,128)S(1)} %slice.1025) | copy-start | bytes 786436
  34.4 11.2 %all-to-all-start.2 = ((f32[128,8,128]{2,1,0:T(8,128)}), f32[128,8,128]{2,1,0:T(8,128)S(1)}, u32[]{:S(2)}, u32[]{:S(2)}) async-start(f32[128,8,128]{2,1,0:T(8,128)} %bitcast.59), calls=%async_computation.2 | async-start | bytes 1048576 | tf_op jit(solution)/shard_map/all_to_all | solution.py:137
  39.6 1.0 slice-start
  45.6 10.3 %all-to-all-start.1 = ((f32[128,8,128]{2,1,0:T(8,128)}), f32[128,8,128]{2,1,0:T(8,128)S(1)}, u32[]{:S(2)}, u32[]{:S(2)}) async-start(f32[128,8,128]{2,1,0:T(8,128)} %bitcast.81), calls=%async_computation.1 | async-start | bytes 1048576 | tf_op jit(solution)/shard_map/all_to_all | solution.py:136
  57.8 1.8 %copy-start.2 = (f32[128,512]{1,0:T(8,128)S(1)}, f32[128,512]{1,0:T(8,128)}, u32[]{:S(2)}) copy-start(f32[128,512]{1,0:T(8,128)} %slice.1118) | copy-start | bytes 786436
  79.4 27.0 %copy-start.4 = (f32[128,8,128]{2,1,0:T(8,128)S(1)}, f32[128,8,128]{2,1,0:T(8,128)}, u32[]{:S(2)}) copy-start(f32[128,8,128]{2,1,0:T(8,128)} %param.4) | copy-start | bytes 1572868
  79.8 26.9 %copy-start = (f32[128,8,128]{2,1,0:T(8,128)S(1)}, f32[128,8,128]{2,1,0:T(8,128)}, u32[]{:S(2)}) copy-start(f32[128,8,128]{2,1,0:T(8,128)} %param.5) | copy-start | bytes 1572868
  106.7 24.8 %copy-start.1 = (f32[128,8,128]{2,1,0:T(8,128)}, f32[128,8,128]{2,1,0:T(8,128)S(1)}, u32[]{:S(2)}) copy-start(f32[128,8,128]{2,1,0:T(8,128)S(1)} %bitcast_add_fusion) | copy-start | bytes 1572868
  106.9 5.8 %collective-permute-start.15 = (f32[2,128,1,128]{3,2,1,0:T(1,128)S(1)}, f32[2,128,1,128]{3,2,1,0:T(1,128)S(1)}, u32[]{:S(2)}, u32[]{:S(2)}) collective-permute-start(f32[2,128,1,128]{3,2,1,0:T(1,128)S(1)} %get-tuple-element.31), channel_id=1, source_target_pairs={{0,2},{2,4},{4,6},{6,8},{8,10},{10,12},{12,14},{14,16},{16,18},{18... | collective-permute-start | bytes 393224 | tf_op jit(solution)/shard_map/ppermute | solution.py:33
  110.5 7.2 %collective-permute-start.16 = (f32[2,128,1,128]{3,2,1,0:T(1,128)S(1)}, f32[2,128,1,128]{3,2,1,0:T(1,128)S(1)}, u32[]{:S(2)}, u32[]{:S(2)}) collective-permute-start(f32[2,128,1,128]{3,2,1,0:T(1,128)S(1)} %get-tuple-element.32), channel_id=1, source_target_pairs={{2,0},{4,2},{6,4},{8,6},{10,8},{12,10},{14,12},{16,14},{18,16},{20... | collective-permute-start | bytes 393224 | tf_op jit(solution)/shard_map/ppermute | solution.py:35
  122.3 3.9 %collective-permute-start.17 = (f32[2,128,10,1]{1,0,3,2:T(2,128)S(1)}, f32[2,128,10,1]{1,0,3,2:T(2,128)S(1)}, u32[]{:S(2)}, u32[]{:S(2)}) collective-permute-start(f32[2,128,10,1]{1,0,3,2:T(2,128)S(1)} %copy.551), channel_id=1, source_target_pairs={{0,1},{2,3},{4,5},{6,7},{8,9},{10,11},{12,13},{14,15},{16,17},{18,... | collective-permute-start | bytes 30728 | tf_op jit(solution)/shard_map/ppermute | solution.py:33
  125.0 4.4 %collective-permute-start.18 = (f32[2,128,10,1]{1,0,3,2:T(2,128)S(1)}, f32[2,128,10,1]{1,0,3,2:T(2,128)S(1)}, u32[]{:S(2)}, u32[]{:S(2)}) collective-permute-start(f32[2,128,10,1]{1,0,3,2:T(2,128)S(1)} %copy.552), channel_id=1, source_target_pairs={{1,0},{3,2},{5,4},{7,6},{9,8},{11,10},{13,12},{15,14},{17,16},{19,... | collective-permute-start | bytes 30728 | tf_op jit(solution)/shard_map/ppermute | solution.py:35
  136.7 1.8 %copy-start.5 = (f32[128,8,128]{2,1,0:T(8,128)S(1)}, f32[128,8,128]{2,1,0:T(8,128)}, u32[]{:S(2)}) copy-start(f32[128,8,128]{2,1,0:T(8,128)} %param.6) | copy-start | bytes 1572868
